TPU v7x, 256 devices: a whole 4x4x8 slice. The times are simulated.
256 devices in a mesh: sensor: 8 (over z_lo, x), param: 32 (over z_hi, y, core).
Axes of the slice: x: 4, y: 4, z: 8 (z_hi: 4, z_lo: 2; z = z_hi * 2 + z_lo), core: 2. Of those that a mesh axis runs over, the one named last changes fastest.
Arguments:
- histories: bfloat16 [2048, 6, 256], P(('param', 'sensor')), may hold values from -6 to 6
- kernel: bfloat16 [512, 2048, 256], P('sensor', 'param'), may hold values from -0.015625 to 0.015625
- noise_weight: float32 [512, 256], P('sensor'), may hold values from 0.5 to 8
Outputs:
- hessian_action: float32 [2048, 6, 256], P(('param', 'sensor'))
All inputs are finite; a program needn't handle non-finite values.
Results may differ from a plain program's by a relative error of at most 0.0027.
Values may be sent and summed in bfloat16 or wider, within the bound.
A program may use at most 64 MiB of HBM per device.

v0:
```python
import jax
import jax.numpy as jnp
from jax import lax
from jax.sharding import PartitionSpec as P

TAPS_BLOCK = 16


def forward_terms(taps_all, piece):
    length = piece.shape[2]
    padded = jnp.pad(piece, ((0, 0), (0, 0), (length, 0)))

    def forward_step(block_index, total):
        first = block_index * TAPS_BLOCK

        def forward_shifted_one(offset):
            return lax.dynamic_slice_in_dim(padded, length - first - offset, length, 2)

        shifted = jax.vmap(forward_shifted_one)(jnp.arange(TAPS_BLOCK, dtype=jnp.int32))
        taps = lax.dynamic_slice_in_dim(taps_all, first, TAPS_BLOCK, 2)
        return total + jnp.einsum(
            "ijk,kjvt->ivt", taps, shifted, preferred_element_type=jnp.float32
        )

    start_total = jnp.zeros((taps_all.shape[0], piece.shape[1], length), jnp.float32)
    return lax.fori_loop(0, length // TAPS_BLOCK, forward_step, start_total)


def adjoint_terms(taps_all, weighted):
    length = weighted.shape[2]
    padded = jnp.pad(weighted, ((0, 0), (0, 0), (0, length)))

    def adjoint_step(block_index, total):
        first = block_index * TAPS_BLOCK

        def adjoint_shifted_one(offset):
            return lax.dynamic_slice_in_dim(padded, first + offset, length, 2)

        shifted = jax.vmap(adjoint_shifted_one)(jnp.arange(TAPS_BLOCK, dtype=jnp.int32))
        taps = lax.dynamic_slice_in_dim(taps_all, first, TAPS_BLOCK, 2)
        return total + jnp.einsum(
            "ijk,kivs->jvs", taps, shifted, preferred_element_type=jnp.float32
        )

    start_total = jnp.zeros((taps_all.shape[1], weighted.shape[1], length), jnp.float32)
    return lax.fori_loop(0, length // TAPS_BLOCK, adjoint_step, start_total)


def shards(histories, kernel, noise_weight):
    taps_all = kernel
    partial_data = forward_terms(taps_all, lax.all_gather(histories, "sensor", axis=0, tiled=True))
    predicted = lax.psum(partial_data, "param")
    weighted = (noise_weight[:, None, :] * predicted).astype(jnp.bfloat16)
    taps_all = kernel
    return lax.psum_scatter(
        adjoint_terms(taps_all, weighted), "sensor", scatter_dimension=0, tiled=True
    )


def solution(mesh):
    in_specs = (P(("param", "sensor"), None, None), P("sensor", "param", None), P("sensor", None))
    out_specs = P(("param", "sensor"), None, None)
    return jax.shard_map(shards, mesh=mesh, in_specs=in_specs, out_specs=out_specs, check_vma=False)
```

profile of v0, /device:TPU:1, one launch (start us, length us, event | category | flops | bytes accessed | tf_op | source)
XLA Modules:
  0.0 713.3 jit_solution(16883173948802724735)
XLA Ops:
  6.5 7.4 %copy.14 = bf16[64,64,256]{1,0,2:T(8,128)(2,1)} copy(bf16[64,64,256]{2,1,0:T(8,128)(2,1)} %param.8) | data formatting | bytes 4194304
  13.9 24.0 %all_gather.3 = bf16[64,6,256]{2,0,1:T(8,128)(2,1)S(1)} all-gather(bf16[8,6,256]{2,0,1:T(8,128)(2,1)S(1)} %copy-done.3), channel_id=1, replica_groups=mesh['sensor'=8,'param'=32] {'sensor'}, dimensions={0}, use_global_device_ids=true | all-gather | bytes 221184 | tf_op jit(solution)/shard_map/all_gather | solution.py:51
  38.4 167.3 %while.28 = (s32[]{:T(128)}, f32[64,6,256]{2,0,1:T(8,128)S(1)}, bf16[64,64,256]{1,0,2:T(8,128)(2,1)}, bf16[64,6,512]{0,1,2:T(8,128)(2,1)S(1)}, s32[]{:T(128)}, /*index=5*/s32[]{:T(128)}, s32[]{:T(128)}, s32[]{:T(128)}) while((s32[]{:T(128)}, f32[64,6,256]{2,0,1:T(8,128)S(1)}, bf16[64,64,256]{1,0,2:T(8,128)(2,1)}, ...), condition=%wide.region_1.2_spmd.clone, body=%wide.region_0.1_spmd.clone.sunk | while | flops 201523296 | bytes 15729057 | solution.py:26
  38.5 4.9 gather_fusion
  43.3 5.5 fusion.39
  48.9 4.9 gather_fusion
  53.8 5.5 fusion.39
  59.4 4.9 gather_fusion
  64.3 5.5 fusion.39
  69.8 4.9 gather_fusion
  74.7 5.5 fusion.39
  80.3 4.9 gather_fusion
  85.2 5.5 fusion.39
  95.6 5.5 fusion.39
  101.2 4.9 gather_fusion
  106.1 5.5 fusion.39
  111.7 4.9 gather_fusion
  116.5 5.5 fusion.39
  122.1 4.9 gather_fusion
  127.0 5.5 fusion.39
  132.6 4.9 gather_fusion
  137.5 5.5 fusion.39
  143.0 4.9 gather_fusion
  147.9 5.5 fusion.39
  153.5 4.9 gather_fusion
  158.4 5.5 fusion.39
  164.0 4.9 gather_fusion
  168.8 5.5 fusion.39
  174.4 4.9 gather_fusion
  179.3 5.5 fusion.39
  184.9 4.9 gather_fusion
  189.7 5.5 fusion.39
  195.3 4.9 gather_fusion
  200.2 5.5 fusion.39
  207.2 8.0 %copy.17 = bf16[64,64,256]{0,1,2:T(8,128)(2,1)} copy(bf16[64,64,256]{2,1,0:T(8,128)(2,1)S(1)} %copy-done) | data formatting | bytes 4194304
  215.4 287.2 %all-reduce.6.cloned.1.call-done = f32[64,6,256]{0,1,2:T(8,128)} async-done(((f32[64,6,256]{0,1,2:T(8,128)}), f32[64,6,256]{0,1,2:T(8,128)}) %all-reduce.6.cloned.1.call-update) | async-done | bytes 393232 | tf_op jit(solution)/shard_map/psum | solution.py:52
  504.2 167.3 %while.29 = (s32[]{:T(128)}, f32[64,6,256]{2,0,1:T(8,128)S(1)}, bf16[64,64,256]{0,1,2:T(8,128)(2,1)}, bf16[64,6,512]{0,1,2:T(8,128)(2,1)S(1)}, s32[]{:T(128)}, /*index=5*/s32[]{:T(128)}, s32[]{:T(128)}, s32[]{:T(128)}) while((s32[]{:T(128)}, f32[64,6,256]{2,0,1:T(8,128)S(1)}, bf16[64,64,256]{0,1,2:T(8,128)(2,1)}, ...), condition=%wide.region_4.5_spmd.clone, body=%wide.region_3.4_spmd.clone.sunk | while | flops 201523296 | bytes 15729045 | solution.py:46
  504.2 4.9 gather_fusion.1
  509.1 5.5 fusion.43
  514.7 4.9 gather_fusion.1
  519.6 5.5 fusion.43
  525.1 4.9 gather_fusion.1
  530.0 5.5 fusion.43
  535.6 4.9 gather_fusion.1
  540.5 5.5 fusion.43
  546.1 4.9 gather_fusion.1
  550.9 5.5 fusion.43
  556.5 4.9 gather_fusion.1
  561.4 5.5 fusion.43
  567.0 4.9 gather_fusion.1
  571.8 5.5 fusion.43
  577.4 4.9 gather_fusion.1
  582.3 5.5 fusion.43
  587.9 4.9 gather_fusion.1
  592.8 5.5 fusion.43
  598.3 4.9 gather_fusion.1
  603.2 5.5 fusion.43
  613.7 5.5 fusion.43
  624.1 5.5 fusion.43
  634.6 5.5 fusion.43
  645.0 5.5 fusion.43
  655.5 5.5 fusion.43
  666.0 5.5 fusion.43
  672.3 34.2 %reduce-scatter.2.cloned.1.call-done = f32[8,6,256]{2,0,1:T(8,128)} async-done(((f32[64,6,256]{2,0,1:T(8,128)}), f32[8,6,256]{2,0,1:T(8,128)}) %reduce-scatter.2.cloned.1.call-update) | async-done | bytes 49168 | tf_op jit(solution)/shard_map/reduce_scatter | solution.py:55
  (59 shorter events, 38.8 us)
Async XLA Ops:
  6.5 7.4 %copy-start.3 = (bf16[8,6,256]{2,0,1:T(8,128)(2,1)S(1)}, bf16[8,6,256]{2,0,1:T(8,128)(2,1)}, u32[]{:S(2)}) copy-start(bf16[8,6,256]{2,0,1:T(8,128)(2,1)} %param.7) | copy-start | bytes 73732
  6.5 496.1 %all-reduce.6.cloned.1.call-start = ((), (), s32[]{:S(2)}) async-start(), calls=%async_computation.1 | async-start | bytes 2097152 | tf_op jit(solution)/shard_map/psum | solution.py:52
  38.4 168.8 %copy-start = (bf16[64,64,256]{2,1,0:T(8,128)(2,1)S(1)}, bf16[64,64,256]{2,1,0:T(8,128)(2,1)}, u32[]{:S(2)}) copy-start(bf16[64,64,256]{2,1,0:T(8,128)(2,1)} %param.8) | copy-start | bytes 6291460
  205.8 9.5 %copy-start.2 = (f32[64,256]{1,0:T(8,128)S(1)}, f32[64,256]{1,0:T(8,128)}, u32[]{:S(2)}) copy-start(f32[64,256]{1,0:T(8,128)} %param.9) | copy-start | bytes 196612
  207.2 499.3 %reduce-scatter.2.cloned.1.call-start = ((), (), s32[]{:S(2)}) async-start(), calls=%async_computation.2 | async-start | bytes 442368 | tf_op jit(solution)/shard_map/reduce_scatter | solution.py:55
  671.5 0.8 copy-start.1
Sparse Core Ops, SparseCore 0:
  207.3 295.2 all-reduce.5
  672.4 34.0 reduce-scatter.1
where the time goes:
time: 718 us; the launch traced here: 713 us
  waiting for transfers between devices  321 us (45%)
  matrix products  177 us (25%)
  local copies, waits for them, and re-layouts  174 us (24%)
  blocking collectives  24 us (3%)
  between operations  13.5 us (2%)
    psum x1, waiting for transfers between devices, shards(): predicted = lax.psum(partial_data, 'param')  287 us
    dot_general x16, matrix products, adjoint_step(): jnp.einsum('ijk,kivs->jvs', taps, shifted, preferred_element_type=jnp.flo...  88.6 us
    dot_general x16, matrix products, forward_step(): jnp.einsum('ijk,kjvt->ivt', taps, shifted, preferred_element_type=jnp.flo...  88.6 us
    gather x16, local copies, waits for them, and re-layouts, forward_shifted_one(): return lax.dynamic_slice_in_dim(padded, length - first - offset, length, 2)  78 us
    gather x16, local copies, waits for them, and re-layouts, adjoint_shifted_one(): return lax.dynamic_slice_in_dim(padded, first + offset, length, 2)  78 us
    reduce_scatter x1, waiting for transfers between devices, shards(): lax.psum_scatter(adjoint_terms(taps_all, weighted), 'sensor', scatter_dim...  34.2 us
    all_gather x1, blocking collectives, shards(): lax.all_gather(histories, 'sensor', axis=0, tiled=True)  24 us
    unnamed x12, local copies, waits for them, and re-layouts  16.6 us
  transfers between devices with their start and end apart: 2, of which 2 were waited for; matrix products, arithmetic and copies ran while one was open for 1% of the time, Pallas kernels for 0%

commit v1 on v0

v1 whole, which is shorter than its diff:
```python
import jax
import jax.numpy as jnp
from jax import lax
from jax.experimental import pallas as pl
from jax.experimental.pallas import tpu as pltpu
from jax.sharding import PartitionSpec as P

F32, BF16 = jnp.float32, jnp.bfloat16
MESH = pl.DeviceIdType.MESH


def lane_of(rows):
    return lax.broadcasted_iota(jnp.int32, (rows, 128), 1)


def spread(xs):
    lane = lane_of(xs[0].shape[0])
    for s in (1, 2, 4):
        low = (lane & s) == 0
        new = list(xs)
        for a in range(8):
            if not a & s:
                new[a] = jnp.where(low, xs[a], pltpu.roll(xs[a | s], s, 1))
                new[a | s] = jnp.where(low, pltpu.roll(xs[a], 128 - s, 1), xs[a | s])
        xs = new
    return xs


def put_taps(a_ref, q, h, g, xs):
    ys = spread(xs)
    col = pl.ds(pl.multiple_of(h * 1024 + g * 128, 128), 128)
    for c in range(8):
        row = pl.multiple_of(c * 32 + 16 * (q % 2), 16)
        a_ref[q // 2, pl.ds(row, 16), col] = ys[c].astype(BF16)


def forward_taps(k_ref, wide_ref, a_ref):
    @pl.loop(0, 64)
    def _(i):
        for h in range(2):
            wide_ref[h, pl.ds(i * 64, 64), :] = k_ref[i, :, 128 * h : 128 * h + 128].astype(F32)

    for h in range(2):

        @pl.loop(0, 32)
        def _(step):
            g, q = step // 4, step % 4
            put_taps(
                a_ref, q, h, g, [wide_ref[h, pl.ds(q * 1024 + 8 * g + j, 16, stride=64), :] for j in range(8)]
            )


def adjoint_taps(k_ref, a_ref, h):
    @pl.loop(0, 32)
    def _(step):
        g, q = step // 4, step % 4
        row = pl.ds(pl.multiple_of(16 * q, 16), 16)
        put_taps(a_ref, q, h, g, [k_ref[8 * g + i, row, 128 * h : 128 * h + 128].astype(F32) for i in range(8)])


def put_shifts(t_ref, g, v, first, second):
    col = pl.ds(v * 128, 128)
    for q in range(8):
        row = pl.multiple_of(g * 128 + 16 * q, 16)
        t_ref[pl.ds(row, 16), col] = jnp.concatenate(first[2 * q : 2 * q + 2], 0).astype(BF16)
        t_ref[pl.ds(1024 + row, 16), col] = jnp.concatenate(second[2 * q : 2 * q + 2], 0).astype(BF16)


def later(lo, hi, s):
    if s == 0:
        return lo, hi
    lane = lane_of(lo.shape[0])
    a, b = pltpu.roll(lo, s, 1), pltpu.roll(hi, s, 1)
    return jnp.where(lane < s, 0.0, a), jnp.where(lane < s, a, b)


def earlier(lo, hi, s):
    if s == 0:
        return lo, hi
    lane = lane_of(lo.shape[0])
    a, b = pltpu.roll(lo, 128 - s, 1), pltpu.roll(hi, 128 - s, 1)
    return jnp.where(lane < 128 - s, a, b), jnp.where(lane < 128 - s, b, 0.0)


def forward_shifts(t_ref, g, v, lo, hi):
    pairs = [later(lo, hi, 8 * l) for l in range(16)]
    put_shifts(t_ref, g, v, [b for _, b in pairs], [a for a, _ in pairs])


def adjoint_shifts(t_ref, g, v, lo, hi):
    pairs = [earlier(lo, hi, 8 * l) for l in range(16)]
    put_shifts(t_ref, g, v, [a for a, _ in pairs], [b for _, b in pairs])


def products(a_ref, half, t_ref, vp, long_ref, short_ref):
    col = pl.ds(pl.multiple_of(vp * 256, 256), 256)
    long_ref[...] = jnp.dot(a_ref[half], t_ref[:, col], preferred_element_type=F32)
    short_ref[...] = jnp.dot(a_ref[half, :, :1024], t_ref[1024:, col], preferred_element_type=F32)


def folded(shift, lo_ref, hi_ref, r, k):
    col = slice(128 * k, 128 * k + 128)
    lo = hi = None
    for c in range(8):
        row = pl.ds(c * 32 + 8 * r, 8)
        a, b = shift(lo_ref[row, col], hi_ref[row, col], c)
        lo, hi = (a, b) if lo is None else (lo + a, hi + b)
    return lo, hi


def body(
    k_hbm, hist_hbm, noise_hbm, out_ref,
    k_ref, hist_ref, noise_ref, wide_ref, a1_ref, a2_ref, t_ref, long_ref, short_ref,
    hb, ybuf, yrecv, ystage, zbuf, zrecv, wall, gf, gmsg, grecv,
    load_sem, h_send, h_recv, c_send, c_recv, y_send, y_recv, z_send, z_recv,
    wz_send, wz_recv, wy_send, wy_recv, wc_send, wc_recv, g_send, g_recv,
):
    ms, mp = lax.axis_index("sensor"), lax.axis_index("param")
    zh, y, core = mp // 8, (mp // 2) % 4, mp % 2

    def sensor_at(s):
        return {"sensor": s, "param": mp}

    def param_at(z_, y_, core_):
        return {"sensor": ms, "param": z_ * 8 + y_ * 2 + core_}

    loads = [
        pltpu.make_async_copy(hist_hbm, hist_ref, load_sem.at[0]),
        pltpu.make_async_copy(k_hbm, k_ref, load_sem.at[1]),
        pltpu.make_async_copy(noise_hbm, noise_ref, load_sem.at[2]),
    ]
    for load in loads:
        load.start()

    barrier = pltpu.get_barrier_semaphore()
    peers = [sensor_at((ms + k) % 8) for k in range(1, 8)]
    peers += [param_at(zh, y, 1 - core)]
    peers += [param_at(zh, (y + k) % 4, core) for k in range(1, 4)]
    peers += [param_at((zh + k) % 4, y, core) for k in range(1, 4)]
    for peer in peers:
        pl.semaphore_signal(barrier, inc=1, device_id=peer, device_id_type=MESH)

    loads[0].wait()
    own = hist_ref[...].astype(F32)
    hb[ms] = jnp.concatenate([own[:, v, :] for v in range(6)], 0).astype(BF16)
    pl.semaphore_wait(barrier, 14)

    def send(src, dst, send_sem, recv_sem, peer):
        copy = pltpu.make_async_remote_copy(
            src_ref=src, dst_ref=dst, send_sem=send_sem, recv_sem=recv_sem, device_id=peer, device_id_type=MESH
        )
        copy.start()
        return copy

    def arrive(dst, recv_sem):
        pltpu.make_async_remote_copy(
            src_ref=dst, dst_ref=dst, send_sem=recv_sem, recv_sem=recv_sem, device_id=sensor_at((ms + 1) % 8),
            device_id_type=MESH,
        ).wait_recv()

    sent = []
    for k in (2, 6, 1, 3, 5, 7, 4):
        sent.append(send(hb.at[ms], hb.at[ms], h_send.at[k], h_recv.at[ms], sensor_at((ms + k) % 8)))

    loads[1].wait()
    forward_taps(k_ref, wide_ref, a1_ref)

    @pl.loop(0, 8)
    def _(k):
        s = (ms + k) % 8

        @pl.when(k > 0)
        def _():
            arrive(hb.at[s], h_recv.at[s])

        block = hb[s].astype(F32)
        for v in range(6):
            forward_shifts(t_ref, s, v, block[8 * v : 8 * v + 8, :128], block[8 * v : 8 * v + 8, 128:])

    for part in range(2):
        half = core if part else 1 - core

        @pl.loop(0, 3)
        def _(vp):
            products(a1_ref, half, t_ref, vp, long_ref, short_ref)
            for r in range(4):
                for k in range(2):
                    lo, hi = folded(later, short_ref, long_ref, r, k)
                    ybuf[part, r, :, pl.ds(pl.multiple_of(256 * vp + 128 * k, 128), 128)] = lo
                    ybuf[part, r, :, pl.ds(pl.multiple_of(768 + 256 * vp + 128 * k, 128), 128)] = hi

        if part == 0:
            sent.append(send(ybuf.at[0], yrecv, c_send, c_recv, param_at(zh, y, 1 - core)))

    arrive(yrecv, c_recv)
    for k in (2, 1, 3):
        to = (y + k) % 4
        ybuf[1, to] = ybuf[1, to] + yrecv[to]
        sent.append(send(ybuf.at[1, to], ystage.at[y], y_send.at[k], y_recv.at[y], param_at(zh, to, core)))

    adjoint_taps(k_ref, a2_ref, 0)

    total = ybuf[1, y] + yrecv[y]
    for k in (1, 3, 2):
        at = (y + k) % 4
        arrive(ystage.at[at], y_recv.at[at])
        total = total + ystage[at]
    for z in range(4):
        zbuf[z] = total[:, 384 * z : 384 * z + 384]
    for k in (2, 1, 3):
        to = (zh + k) % 4
        sent.append(send(zbuf.at[to], zrecv.at[zh], z_send.at[k], z_recv.at[zh], param_at(to, y, core)))
    loads[2].wait()
    group = core * 4 + y
    noise = noise_ref[pl.ds(pl.multiple_of(8 * group, 8), 8), pl.ds(pl.multiple_of(128 * (zh // 2), 128), 128)]
    piece = zbuf[zh]
    for k in (1, 3, 2):
        at = (zh + k) % 4
        arrive(zrecv.at[at], z_recv.at[at])
        piece = piece + zrecv[at]
    tiles = [piece[:, 128 * k : 128 * k + 128] * noise for k in range(3)]
    tiles.append(jnp.zeros_like(noise))
    wall[group * 4 + zh] = jnp.concatenate(
        [jnp.concatenate(tiles[:2], 1), jnp.concatenate(tiles[2:], 1)], 0
    ).astype(BF16)
    for k in (2, 1, 3):
        here = group * 4 + zh
        sent.append(
            send(wall.at[here], wall.at[here], wz_send.at[k], wz_recv.at[zh], param_at((zh + k) % 4, y, core))
        )

    adjoint_taps(k_ref, a2_ref, 1)

    for k in (1, 3, 2):
        at = (zh + k) % 4
        arrive(wall.at[group * 4 + at], wz_recv.at[at])
    block = wall.at[pl.ds(group * 4, 4)]
    for k in (2, 1, 3):
        sent.append(send(block, block, wy_send.at[k], wy_recv.at[y], param_at(zh, (y + k) % 4, core)))
    sent.append(send(block, block, wc_send.at[y], wc_recv.at[y], param_at(zh, y, 1 - core)))

    def weighted_shifts(g):
        pieces = [wall[g * 4 + z].astype(F32) for z in range(4)]
        for v in range(6):
            row, col = 8 * (v % 3 // 2), 128 * (v % 3 % 2)
            lo, hi = [pieces[z][row : row + 8, col : col + 128] for z in (v // 3, 2 + v // 3)]
            adjoint_shifts(t_ref, g, v, lo, hi)

    @pl.loop(0, 8)
    def _(step):
        at = (y + step) % 4
        mine = step < 4
        g = jnp.where(mine, core, 1 - core) * 4 + at
        here = wall.at[pl.ds(g * 4, 4)]

        @pl.when((step > 0) & mine)
        def _():
            arrive(here, wy_recv.at[at])
            send(here, here, wc_send.at[at], wc_recv.at[at], param_at(zh, y, 1 - core))

        @pl.when(step >= 4)
        def _():
            arrive(here, wc_recv.at[at])

        weighted_shifts(g)

    for part in range(2):
        half = ms // 4 if part else 1 - ms // 4

        @pl.loop(0, 3)
        def _(vp):
            products(a2_ref, half, t_ref, vp, long_ref, short_ref)
            for r in range(4):
                for k in range(2):
                    lo, hi = folded(earlier, long_ref, short_ref, r, k)
                    gf[part, r, :, pl.ds(pl.multiple_of(256 * vp + 128 * k, 128), 128)] = jnp.concatenate([lo, hi], 0)

        for k in (2, 1, 3, 0):
            to = (ms + k) % 4
            if part and k == 0:
                continue
            slot = half * 4 + to
            gmsg[slot] = gf[part, to].astype(BF16)
            sent.append(
                send(gmsg.at[slot], grecv.at[ms], g_send.at[4 * part + k], g_recv.at[ms], sensor_at(slot))
            )

    total = gf[1, ms % 4]
    for k in range(1, 8):
        at = (ms + k) % 8
        arrive(grecv.at[at], g_recv.at[at])
        total = total + grecv[at].astype(F32)
    for v in range(6):
        for t in range(2):
            out_ref[:, v, 128 * t : 128 * t + 128] = total[8 * t : 8 * t + 8, 128 * v : 128 * v + 128]

    for copy in sent:
        copy.wait_send()
    for k in range(1, 4):
        at = (y + k) % 4
        here = wall.at[pl.ds((core * 4 + at) * 4, 4)]
        pltpu.make_async_remote_copy(
            src_ref=here, dst_ref=here, send_sem=wc_send.at[at], recv_sem=wc_recv.at[at],
            device_id=param_at(zh, y, 1 - core), device_id_type=MESH,
        ).wait_send()


def shards(histories, kernel, noise_weight):
    V, S = pltpu.VMEM, pltpu.SemaphoreType.DMA
    return pl.pallas_call(
        body,
        out_shape=jax.ShapeDtypeStruct((8, 6, 256), F32),
        in_specs=[pl.BlockSpec(memory_space=pl.ANY)] * 3,
        out_specs=pl.BlockSpec(memory_space=pltpu.VMEM),
        scratch_shapes=[
            V((64, 64, 256), BF16), V((8, 6, 256), BF16), V((64, 256), F32), V((2, 4096, 128), F32),
            V((2, 256, 2048), BF16), V((2, 256, 2048), BF16), V((2048, 768), BF16), V((256, 256), F32),
            V((256, 256), F32),
            V((8, 48, 256), BF16), V((2, 4, 8, 1536), F32), V((4, 8, 1536), F32), V((4, 8, 1536), F32),
            V((4, 8, 384), F32), V((4, 8, 384), F32), V((32, 16, 256), BF16), V((2, 4, 16, 768), F32),
            V((8, 16, 768), BF16), V((8, 16, 768), BF16),
            S((3,)), S((8,)), S((8,)), S(()), S(()), S((4,)), S((4,)), S((4,)), S((4,)),
            S((4,)), S((4,)), S((4,)), S((4,)), S((4,)), S((4,)), S((8,)), S((8,)),
        ],
        compiler_params=pltpu.CompilerParams(
            collective_id=0, has_side_effects=True, vmem_limit_bytes=48 * 2**20
        ),
        cost_estimate=pl.CostEstimate(flops=4831838208, bytes_accessed=2300000, transcendentals=0),
        name="hessian",
    )(kernel, histories, noise_weight)


def solution(mesh):
    in_specs = (P(("param", "sensor"), None, None), P("sensor", "param", None), P("sensor", None))
    out_specs = P(("param", "sensor"), None, None)
    return jax.shard_map(shards, mesh=mesh, in_specs=in_specs, out_specs=out_specs, check_vma=False)
```

time: 718 us -> 69.2 us (0.10)
  waiting for transfers between devices: 321 us -> 0 us
  matrix products: 177 us -> 0 us
  local copies, waits for them, and re-layouts: 174 us -> 3.81 us
  Pallas kernels: 0 us -> 65.2 us
  blocking collectives: 24 us -> 0 us
  between operations: 13.5 us -> 0.02 us
    psum x1 -> x0, waiting for transfers between devices: 287 us -> none  [shards(): predicted = lax.psum(partial_data, 'param')]
    dot_general x32 -> x0, matrix products: 177 us -> none  [the longest x16 88.6 us: adjoint_step(): jnp.einsum('ijk,kivs->jvs', taps, shifted, preferred_element_type=jnp.flo...]
    gather x32 -> x0, local copies, waits for them, and re-layouts: 156 us -> none  [the longest x16 78 us: forward_shifted_one(): return lax.dynamic_slice_in_dim(padded, length - first - offset, length, 2)]
    pallas_call x0 -> x1, Pallas kernels: none -> 65.2 us  [shards(): pl.pallas_call(body, out_shape=jax.ShapeDtypeStruct((8, 6, 256), F32), in...]
    reduce_scatter x1 -> x0, waiting for transfers between devices: 34.2 us -> none  [shards(): lax.psum_scatter(adjoint_terms(taps_all, weighted), 'sensor', scatter_dim...]
    all_gather x1 -> x0, blocking collectives: 24 us -> none  [shards(): lax.all_gather(histories, 'sensor', axis=0, tiled=True)]
    unnamed x12 -> x5, local copies, waits for them, and re-layouts: 16.6 us -> 3.17 us
  transfers between devices with their start and end apart: 2 -> 0, of which waited for: 2 -> 0; matrix products, arithmetic and copies ran while one was open for 1% -> 0% of each run, Pallas kernels for 0% -> 0%
where the time goes in v1:
time: 69.2 us; the launch traced here: 69 us
  Pallas kernels  65.2 us (94%)
  local copies, waits for them, and re-layouts  3.81 us (6%)
    pallas_call x1, Pallas kernels, shards(): pl.pallas_call(body, out_shape=jax.ShapeDtypeStruct((8, 6, 256), F32), in...  65.2 us
    unnamed x5, local copies, waits for them, and re-layouts  3.17 us

profile of v1, /device:TPU:1, one launch (start us, length us, event | category | flops | bytes accessed | tf_op | source)
XLA Modules:
  0.0 69.0 jit_solution(14054704609374675259)
XLA Ops:
  0.0 0.7 %copy.4.hist_hbm = bf16[8,6,256]{2,1,0:T(8,128)(2,1)S(1)} copy(bf16[8,6,256]{2,0,1:T(8,128)(2,1)} %param.3) | data formatting | bytes 49152 | tf_op args[0]
  0.7 0.0 copy-start
  0.8 1.6 %copy-done = bf16[64,64,256]{2,1,0:T(8,128)(2,1)S(1)} copy-done((bf16[64,64,256]{2,1,0:T(8,128)(2,1)S(1)}, bf16[64,64,256]{2,1,0:T(8,128)(2,1)}, u32[]{:S(2)}) %copy-start) | copy-done | bytes 2097176
  2.3 0.0 copy-start.1
  2.3 0.8 %copy-done.1 = f32[64,256]{1,0:T(8,128)S(1)} copy-done((f32[64,256]{1,0:T(8,128)S(1)}, f32[64,256]{1,0:T(8,128)}, u32[]{:S(2)}) %copy-start.1) | copy-done | bytes 65560
  3.2 65.2 %hessian.1 = f32[8,6,256]{2,1,0:T(8,128)S(1)} custom-call(bf16[64,64,256]{2,1,0:T(8,128)(2,1)S(1)} %copy-done, bf16[8,6,256]{2,1,0:T(8,128)(2,1)S(1)} %copy.4.hist_hbm, f32[64,256]{1,0:T(8,128)S(1)} %copy-done.1), custom_call_target="tpu_custom_call" | custom-call | flops 4831838208 | bytes 2300000 | tf_op jit(solution)/shard_map/hessian/pallas_call | solution.py:310
  68.4 0.6 copy.5
Async XLA Ops:
  0.7 1.6 %copy-start = (bf16[64,64,256]{2,1,0:T(8,128)(2,1)S(1)}, bf16[64,64,256]{2,1,0:T(8,128)(2,1)}, u32[]{:S(2)}) copy-start(bf16[64,64,256]{2,1,0:T(8,128)(2,1)} %k_hbm.1) | copy-start | bytes 6291460
  2.3 0.8 %copy-start.1 = (f32[64,256]{1,0:T(8,128)S(1)}, f32[64,256]{1,0:T(8,128)}, u32[]{:S(2)}) copy-start(f32[64,256]{1,0:T(8,128)} %noise_hbm.1) | copy-start | bytes 196612

commit v2 on v1

--- a/solution.py
+++ b/solution.py
@@ -13,49 +13,56 @@
     return lax.broadcasted_iota(jnp.int32, (rows, 128), 1)
 
 
-def spread(xs):
-    lane = lane_of(xs[0].shape[0])
-    for s in (1, 2, 4):
-        low = (lane & s) == 0
-        new = list(xs)
-        for a in range(8):
-            if not a & s:
-                new[a] = jnp.where(low, xs[a], pltpu.roll(xs[a | s], s, 1))
-                new[a | s] = jnp.where(low, pltpu.roll(xs[a], 128 - s, 1), xs[a | s])
-        xs = new
-    return xs
-
-
-def put_taps(a_ref, q, h, g, xs):
-    ys = spread(xs)
-    col = pl.ds(pl.multiple_of(h * 1024 + g * 128, 128), 128)
-    for c in range(8):
-        row = pl.multiple_of(c * 32 + 16 * (q % 2), 16)
-        a_ref[q // 2, pl.ds(row, 16), col] = ys[c].astype(BF16)
-
-
-def forward_taps(k_ref, wide_ref, a_ref):
-    @pl.loop(0, 64)
-    def _(i):
-        for h in range(2):
-            wide_ref[h, pl.ds(i * 64, 64), :] = k_ref[i, :, 128 * h : 128 * h + 128].astype(F32)
-
-    for h in range(2):
-
-        @pl.loop(0, 32)
-        def _(step):
-            g, q = step // 4, step % 4
-            put_taps(
-                a_ref, q, h, g, [wide_ref[h, pl.ds(q * 1024 + 8 * g + j, 16, stride=64), :] for j in range(8)]
-            )
-
-
-def adjoint_taps(k_ref, a_ref, h):
+def fill_order(order_ref):
+    row, col = [lax.broadcasted_iota(jnp.int32, (128, 1024), d) for d in (0, 1)]
+    low = row & 7
+    target = low * 128 + (row - low)
+
+    @pl.loop(0, 8)
+    def _(j):
+        here = jnp.where(col == target + j, 1.0, 0.0).astype(BF16)
+        order_ref[pl.ds(pl.multiple_of(j * 128, 128), 128), :] = here
+
+
+def put_taps(x, order_ref, a_ref, h, n):
+    ys = jnp.dot(x, order_ref[:, pl.ds(pl.multiple_of(n * 256, 256), 256)], preferred_element_type=F32)
+    for half in range(2):
+        for g in range(8):
+            for c in range(2):
+                part = ys[64 * g + 32 * half : 64 * g + 32 * half + 32, 128 * c : 128 * c + 128]
+                row = pl.ds(pl.multiple_of((2 * n + c) * 32, 32), 32)
+                col = pl.ds(pl.multiple_of(h * 1024 + g * 128, 128), 128)
+                a_ref[half, row, col] = part.astype(BF16)
+
+
+def forward_taps(k_ref, wide_ref, x_ref, order_ref, a_ref):
     @pl.loop(0, 32)
     def _(step):
-        g, q = step // 4, step % 4
-        row = pl.ds(pl.multiple_of(16 * q, 16), 16)
-        put_taps(a_ref, q, h, g, [k_ref[8 * g + i, row, 128 * h : 128 * h + 128].astype(F32) for i in range(8)])
+        for u in range(2):
+            i = 2 * step + u
+            for h in range(2):
+                wide_ref[h, pl.ds(pl.multiple_of(i * 72, 8), 64), :] = k_ref[i, :, 128 * h : 128 * h + 128].astype(F32)
+
+    for h in range(2):
+
+        @pl.loop(0, 8)
+        def _(g):
+            row = pl.ds(pl.multiple_of(64 * g, 64), 64)
+            for j in range(8):
+                x_ref[h, row, 128 * j : 128 * j + 128] = wide_ref[h, pl.ds(8 * g + j, 64, stride=72), :].astype(BF16)
+
+    @pl.loop(0, 8)
+    def _(step):
+        put_taps(x_ref[step // 4], order_ref, a_ref, step // 4, step % 4)
+
+
+def adjoint_taps(k_ref, order_ref, a_ref, h):
+    @pl.loop(0, 4)
+    def _(n):
+        x = [
+            jnp.concatenate([k_ref[8 * g + i, :, 128 * h : 128 * h + 128] for g in range(8)], 0) for i in range(8)
+        ]
+        put_taps(jnp.concatenate(x, 1), order_ref, a_ref, h, n)
 
 
 def put_shifts(t_ref, g, v, first, second):
@@ -110,7 +117,7 @@
 
 def body(
     k_hbm, hist_hbm, noise_hbm, out_ref,
-    k_ref, hist_ref, noise_ref, wide_ref, a1_ref, a2_ref, t_ref, long_ref, short_ref,
+    k_ref, noise_ref, wide_ref, x_ref, order_ref, a1_ref, a2_ref, t_ref, long_ref, short_ref,
     hb, ybuf, yrecv, ystage, zbuf, zrecv, wall, gf, gmsg, grecv,
     load_sem, h_send, h_recv, c_send, c_recv, y_send, y_recv, z_send, z_recv,
     wz_send, wz_recv, wy_send, wy_recv, wc_send, wc_recv, g_send, g_recv,
@@ -125,7 +132,7 @@
         return {"sensor": ms, "param": z_ * 8 + y_ * 2 + core_}
 
     loads = [
-        pltpu.make_async_copy(hist_hbm, hist_ref, load_sem.at[0]),
+        pltpu.make_async_copy(hist_hbm, hb.at[ms], load_sem.at[0]),
         pltpu.make_async_copy(k_hbm, k_ref, load_sem.at[1]),
         pltpu.make_async_copy(noise_hbm, noise_ref, load_sem.at[2]),
     ]
@@ -140,9 +147,8 @@
     for peer in peers:
         pl.semaphore_signal(barrier, inc=1, device_id=peer, device_id_type=MESH)
 
+    fill_order(order_ref)
     loads[0].wait()
-    own = hist_ref[...].astype(F32)
-    hb[ms] = jnp.concatenate([own[:, v, :] for v in range(6)], 0).astype(BF16)
     pl.semaphore_wait(barrier, 14)
 
     def send(src, dst, send_sem, recv_sem, peer):
@@ -163,7 +169,7 @@
         sent.append(send(hb.at[ms], hb.at[ms], h_send.at[k], h_recv.at[ms], sensor_at((ms + k) % 8)))
 
     loads[1].wait()
-    forward_taps(k_ref, wide_ref, a1_ref)
+    forward_taps(k_ref, wide_ref, x_ref, order_ref, a1_ref)
 
     @pl.loop(0, 8)
     def _(k):
@@ -198,7 +204,7 @@
         ybuf[1, to] = ybuf[1, to] + yrecv[to]
         sent.append(send(ybuf.at[1, to], ystage.at[y], y_send.at[k], y_recv.at[y], param_at(zh, to, core)))
 
-    adjoint_taps(k_ref, a2_ref, 0)
+    adjoint_taps(k_ref, order_ref, a2_ref, 0)
 
     total = ybuf[1, y] + yrecv[y]
     for k in (1, 3, 2):
@@ -229,7 +235,7 @@
             send(wall.at[here], wall.at[here], wz_send.at[k], wz_recv.at[zh], param_at((zh + k) % 4, y, core))
         )
 
-    adjoint_taps(k_ref, a2_ref, 1)
+    adjoint_taps(k_ref, order_ref, a2_ref, 1)
 
     for k in (1, 3, 2):
         at = (zh + k) % 4
@@ -292,7 +298,7 @@
         total = total + grecv[at].astype(F32)
     for v in range(6):
         for t in range(2):
-            out_ref[:, v, 128 * t : 128 * t + 128] = total[8 * t : 8 * t + 8, 128 * v : 128 * v + 128]
+            out_ref[8 * v : 8 * v + 8, 128 * t : 128 * t + 128] = total[8 * t : 8 * t + 8, 128 * v : 128 * v + 128]
 
     for copy in sent:
         copy.wait_send()
@@ -307,13 +313,13 @@
 
 def shards(histories, kernel, noise_weight):
     V, S = pltpu.VMEM, pltpu.SemaphoreType.DMA
-    return pl.pallas_call(
+    out = pl.pallas_call(
         body,
-        out_shape=jax.ShapeDtypeStruct((8, 6, 256), F32),
-        in_specs=[pl.BlockSpec(memory_space=pl.ANY)] * 3,
+        out_shape=jax.ShapeDtypeStruct((48, 256), F32),
+        in_specs=[pl.BlockSpec(memory_space=pltpu.HBM)] * 3,
         out_specs=pl.BlockSpec(memory_space=pltpu.VMEM),
         scratch_shapes=[
-            V((64, 64, 256), BF16), V((8, 6, 256), BF16), V((64, 256), F32), V((2, 4096, 128), F32),
+            V((64, 64, 256), BF16), V((64, 256), F32), V((2, 4608, 128), F32), V((2, 512, 1024), BF16), V((1024, 1024), BF16),
             V((2, 256, 2048), BF16), V((2, 256, 2048), BF16), V((2048, 768), BF16), V((256, 256), F32),
             V((256, 256), F32),
             V((8, 48, 256), BF16), V((2, 4, 8, 1536), F32), V((4, 8, 1536), F32), V((4, 8, 1536), F32),
@@ -323,11 +329,12 @@
             S((4,)), S((4,)), S((4,)), S((4,)), S((4,)), S((4,)), S((8,)), S((8,)),
         ],
         compiler_params=pltpu.CompilerParams(
-            collective_id=0, has_side_effects=True, vmem_limit_bytes=48 * 2**20
+            collective_id=0, has_side_effects=True, vmem_limit_bytes=60 * 2**20
         ),
         cost_estimate=pl.CostEstimate(flops=4831838208, bytes_accessed=2300000, transcendentals=0),
         name="hessian",
-    )(kernel, histories, noise_weight)
+    )(kernel, histories.transpose(1, 0, 2).reshape(48, 256), noise_weight)
+    return out.reshape(6, 8, 256).transpose(1, 0, 2)
 
 
 def solution(mesh):

time: 69.2 us -> 50.6 us (0.73)
  Pallas kernels: 65.2 us -> 49 us
  local copies, waits for them, and re-layouts: 3.81 us -> 1.42 us
    pallas_call x1, Pallas kernels: 65.2 us -> 49 us  [shards(): pl.pallas_call(body, out_shape=jax.ShapeDtypeStruct((48, 256), F32), in_s...]
    unnamed x5 -> x1, local copies, waits for them, and re-layouts: 3.17 us -> 1.42 us
where the time goes in v2:
time: 50.6 us; the launch traced here: 50.4 us
  Pallas kernels  49 us (97%)
  local copies, waits for them, and re-layouts  1.42 us (3%)
    pallas_call x1, Pallas kernels, shards(): pl.pallas_call(body, out_shape=jax.ShapeDtypeStruct((48, 256), F32), in_s...  49 us
    unnamed x1, local copies, waits for them, and re-layouts  1.42 us

profile of v2, /device:TPU:1, one launch (start us, length us, event | category | flops | bytes accessed | tf_op | source)
XLA Modules:
  0.0 50.4 jit_solution(11012709490265265652)
XLA Ops:
  0.0 49.0 %hessian.1 = f32[48,256]{1,0:T(8,128)} custom-call(bf16[64,64,256]{2,1,0:T(8,128)(2,1)} %k_hbm.1, bf16[48,256]{1,0:T(8,128)(2,1)} %bitcast.7, f32[64,256]{1,0:T(8,128)} %noise_hbm.1), custom_call_target="tpu_custom_call" | custom-call | flops 4831838208 | bytes 2300000 | tf_op jit(solution)/shard_map/hessian/pallas_call | solution.py:316
  49.0 1.4 %copy.5 = f32[8,6,256]{2,0,1:T(8,128)} copy(f32[8,6,256]{2,0,1:T(8,128)} %bitcast.6) | data formatting | bytes 98304

commit v3 on v2

v3 whole, which is shorter than its diff:
```python
import jax
import jax.numpy as jnp
from jax import lax
from jax.experimental import pallas as pl
from jax.experimental.pallas import tpu as pltpu
from jax.sharding import PartitionSpec as P

F32, BF16 = jnp.float32, jnp.bfloat16
MESH = pl.DeviceIdType.MESH


def lane_of(rows):
    return lax.broadcasted_iota(jnp.int32, (rows, 128), 1)


def fill_order(order_ref):
    row, col = [lax.broadcasted_iota(jnp.int32, (128, 1024), d) for d in (0, 1)]
    low = row & 7
    target = low * 128 + (row - low)

    @pl.loop(0, 8)
    def _(j):
        here = jnp.where(col == target + j, 1.0, 0.0).astype(BF16)
        order_ref[pl.ds(pl.multiple_of(j * 128, 128), 128), :] = here


def reordered(x, order_ref, n):
    return jnp.dot(x, order_ref[:, pl.ds(pl.multiple_of(n * 256, 256), 256)], preferred_element_type=F32)


def forward_taps(k_ref, wide_ref, x_ref, order_ref, a_ref):
    for h in range(2):

        @pl.loop(0, 8)
        def _(g):
            row = pl.ds(pl.multiple_of(64 * g, 64), 64)
            for j in range(8):
                x_ref[h, row, 128 * j : 128 * j + 128] = wide_ref[h, pl.ds(8 * g + j, 64, stride=72), :].astype(BF16)

    @pl.loop(0, 8)
    def _(step):
        h, n = step // 4, step % 4
        ys = reordered(x_ref[h], order_ref, n)
        for z in range(4):
            for g in range(8):
                for c in range(2):
                    first = 64 * g + 8 * z
                    part = [ys[r : r + 8, 128 * c : 128 * c + 128] for r in (first, first + 32)]
                    row = pl.ds(pl.multiple_of((2 * n + c) * 16, 16), 16)
                    col = pl.ds(pl.multiple_of(h * 1024 + g * 128, 128), 128)
                    a_ref[z, row, col] = jnp.concatenate(part, 0).astype(BF16)


def adjoint_taps(k_ref, order_ref, a_ref, h):
    @pl.loop(0, 4)
    def _(n):
        x = [
            jnp.concatenate([k_ref[8 * g + i, :, 128 * h : 128 * h + 128] for g in range(8)], 0) for i in range(8)
        ]
        ys = reordered(jnp.concatenate(x, 1), order_ref, n)
        for to in range(2):
            for g in range(8):
                for c in range(2):
                    first = 64 * g + 32 * to
                    row = pl.ds(pl.multiple_of(256 * to + (2 * n + c) * 32, 32), 32)
                    a_ref[g % 4, row, 256 * h + 128 * (g // 4) : 256 * h + 128 * (g // 4) + 128] = ys[
                        first : first + 32, 128 * c : 128 * c + 128
                    ].astype(BF16)


def put_shifts(t_ref, rows, v, series):
    col = pl.ds(v * 128, 128)
    for start, shifted in zip(rows, series):
        for q in range(8):
            row = pl.multiple_of(start + 16 * q, 16)
            t_ref[pl.ds(row, 16), col] = jnp.concatenate(shifted[2 * q : 2 * q + 2], 0).astype(BF16)


def later(lo, hi, s):
    if s == 0:
        return lo, hi
    lane = lane_of(lo.shape[0])
    a, b = pltpu.roll(lo, s, 1), pltpu.roll(hi, s, 1)
    return jnp.where(lane < s, 0.0, a), jnp.where(lane < s, a, b)


def earlier(lo, hi, s):
    if s == 0:
        return lo, hi
    lane = lane_of(lo.shape[0])
    a, b = pltpu.roll(lo, 128 - s, 1), pltpu.roll(hi, 128 - s, 1)
    return jnp.where(lane < 128 - s, a, b), jnp.where(lane < 128 - s, b, 0.0)


def forward_shifts(t_ref, g, v, lo, hi):
    pairs = [later(lo, hi, 8 * l) for l in range(16)]
    put_shifts(t_ref, (1024 + g * 128, g * 128), v, zip(*pairs))


def adjoint_shifts(t_ref, half, v, lo, hi):
    pairs = [earlier(lo, hi, 8 * l) for l in range(16)]
    put_shifts(t_ref, (half * 128, 256 + half * 128), v, zip(*pairs))


def folded(shift, lo_ref, hi_ref, start, stride, v):
    col = slice(128 * v, 128 * v + 128)
    lo = hi = None
    for c in range(8):
        row = pl.ds(start + stride * c, 8)
        a, b = shift(lo_ref[row, col], hi_ref[row, col], c)
        lo, hi = (a, b) if lo is None else (lo + a, hi + b)
    return lo, hi


def body(
    k_hbm, hist_hbm, noise_hbm, out_ref,
    k_ref, noise_ref, wide_ref, x_ref, order_ref, a1_ref, a2_ref, t1_ref, long_ref, short_ref, t2_ref, q0_ref, q1_ref,
    hb, ybuf, yrecv, zrecv, wall, gf, gmsg, grecv,
    load_sem, h_send, h_recv, c_send, c_recv, z_send, z_recv, w_send, w_recv, wc_send, wc_recv, g_send, g_recv,
):
    ms, mp = lax.axis_index("sensor"), lax.axis_index("param")
    zh, y, core = mp // 8, (mp // 2) % 4, mp % 2

    def sensor_at(s):
        return {"sensor": s, "param": mp}

    def param_at(z_, y_, core_):
        return {"sensor": ms, "param": z_ * 8 + y_ * 2 + core_}

    partner = param_at(zh, y, 1 - core)

    pltpu.make_async_copy(hist_hbm, hb.at[ms], load_sem.at[0]).start()
    k_loads = []
    for part in range(4):
        rows = pl.ds(16 * part, 16)
        k_loads.append(pltpu.make_async_copy(k_hbm.at[rows], k_ref.at[rows], load_sem.at[2 + part]))
        k_loads[-1].start()
    pltpu.make_async_copy(noise_hbm, noise_ref, load_sem.at[1]).start()

    barrier = pltpu.get_barrier_semaphore()
    peers = [sensor_at((ms + k) % 8) for k in range(1, 8)]
    peers += [partner]
    peers += [param_at((zh + dz) % 4, (y + dy) % 4, core) for dz in range(4) for dy in range(4) if dz or dy]
    for peer in peers:
        pl.semaphore_signal(barrier, inc=1, device_id=peer, device_id_type=MESH)

    fill_order(order_ref)
    pltpu.make_async_copy(hist_hbm, hb.at[ms], load_sem.at[0]).wait()
    pl.semaphore_wait(barrier, len(peers))

    def send(src, dst, send_sem, recv_sem, peer):
        copy = pltpu.make_async_remote_copy(
            src_ref=src, dst_ref=dst, send_sem=send_sem, recv_sem=recv_sem, device_id=peer, device_id_type=MESH
        )
        copy.start()
        return copy

    def arrive(dst, recv_sem):
        pltpu.make_async_remote_copy(
            src_ref=dst, dst_ref=dst, send_sem=recv_sem, recv_sem=recv_sem, device_id=partner, device_id_type=MESH
        ).wait_recv()

    def sent_off(src, send_sem):
        pltpu.make_async_remote_copy(
            src_ref=src, dst_ref=src, send_sem=send_sem, recv_sem=send_sem, device_id=partner, device_id_type=MESH
        ).wait_send()

    sent = []
    for k in (2, 6, 1, 3, 5, 7, 4):
        sent.append(send(hb.at[ms], hb.at[ms], h_send.at[k], h_recv.at[ms], sensor_at((ms + k) % 8)))

    for part in range(4):
        k_loads[part].wait()

        @pl.loop(8 * part, 8 * part + 8)
        def _(step):
            for u in range(2):
                i = 2 * step + u
                for h in range(2):
                    wide_ref[h, pl.ds(pl.multiple_of(i * 72, 8), 64), :] = k_ref[i, :, 128 * h : 128 * h + 128].astype(F32)

    forward_taps(k_ref, wide_ref, x_ref, order_ref, a1_ref)

    @pl.loop(0, 8)
    def _(k):
        s = (ms + k) % 8

        @pl.when(k > 0)
        def _():
            arrive(hb.at[s], h_recv.at[s])

        block = hb[s].astype(F32)
        for v in range(6):
            forward_shifts(t1_ref, s, v, block[8 * v : 8 * v + 8, :128], block[8 * v : 8 * v + 8, 128:])

    def z_of(b):
        return (zh + jnp.where(b == 0, 2, jnp.where(b == 1, 1, jnp.where(b == 2, 3, 0)))) % 4

    def pass_on(b, dys):
        arrive(yrecv.at[b], c_recv.at[b])
        for dy in dys:
            to = (y + dy) % 4
            ybuf[b, 1, to] = ybuf[b, 1, to] + yrecv[b, to]
            send(
                ybuf.at[b, 1, to], zrecv.at[zh * 4 + y], z_send.at[b, dy], z_recv.at[zh * 4 + y],
                param_at(z_of(b), to, core),
            )

    @pl.loop(0, 4)
    def _(b):
        z = z_of(b)
        long_ref[...] = jnp.dot(a1_ref[z], t1_ref[...], preferred_element_type=F32)
        short_ref[...] = jnp.dot(a1_ref[z, :, :1024], t1_ref[1024:, :], preferred_element_type=F32)
        for half in range(2):
            mine = (half + core + 1) % 2
            for v in range(6):
                lo, hi = folded(later, short_ref, long_ref, 8 * half, 16, v)
                col = slice(128 * (v % 3), 128 * (v % 3) + 128)
                ybuf[b, mine, v // 3, :, col] = lo
                ybuf[b, mine, 2 + v // 3, :, col] = hi
        send(ybuf.at[b, 0], yrecv.at[b], c_send.at[b], c_recv.at[b], partner)

        @pl.when(b > 0)
        def _():
            pass_on(b - 1, (2, 1, 3, 0))

    pass_on(3, (2, 1, 3))

    adjoint_taps(k_ref, order_ref, a2_ref, 0)

    piece = ybuf[3, 1, y] + yrecv[3, y]
    for dz in (2, 1, 3, 0):
        for dy in range(4):
            if dz or dy:
                at = ((zh + dz) % 4) * 4 + (y + dy) % 4
                arrive(zrecv.at[at], z_recv.at[at])
                piece = piece + zrecv[at]

    pltpu.make_async_copy(noise_hbm, noise_ref, load_sem.at[1]).wait()
    group = core * 4 + zh
    noise = noise_ref[pl.ds(pl.multiple_of(8 * group, 8), 8), pl.ds(pl.multiple_of(128 * (y // 2), 128), 128)]
    tiles = [piece[:, 128 * k : 128 * k + 128] * noise for k in range(3)]
    tiles.append(jnp.zeros_like(noise))
    here = group * 4 + y
    wall[here] = jnp.concatenate(
        [jnp.concatenate(tiles[:2], 1), jnp.concatenate(tiles[2:], 1)], 0
    ).astype(BF16)
    for dz in (2, 1, 3, 0):
        for dy in (2, 1, 3, 0):
            if dz or dy:
                peer = param_at((zh + dz) % 4, (y + dy) % 4, core)
                sent.append(send(wall.at[here], wall.at[here], w_send.at[dz * 4 + dy], w_recv.at[zh * 4 + y], peer))

    adjoint_taps(k_ref, order_ref, a2_ref, 1)
    q0_ref[...] = jnp.zeros_like(q0_ref)
    q1_ref[...] = jnp.zeros_like(q1_ref)

    def weighted_shifts(half, z):
        pieces = [wall[(half * 4 + z) * 4 + y_].astype(F32) for y_ in range(4)]
        for v in range(6):
            row, col = 8 * (v % 3 // 2), 128 * (v % 3 % 2)
            lo, hi = [pieces[y_][row : row + 8, col : col + 128] for y_ in (v // 3, 2 + v // 3)]
            adjoint_shifts(t2_ref, half, v, lo, hi)

    def gather(step):
        z = (zh + jnp.where(step == 0, 0, jnp.where(step == 1, 1, jnp.where(step == 2, 3, 2)))) % 4
        for dy in (1, 3, 2, 0):
            at = (y + dy) % 4

            @pl.when((step > 0) | (dy > 0))
            def _():
                arrive(wall.at[(core * 4 + z) * 4 + at], w_recv.at[z * 4 + at])

        block = wall.at[pl.ds((core * 4 + z) * 4, 4)]
        send(block, block, wc_send.at[z], wc_recv.at[z], partner)
        weighted_shifts(core, z)
        other = wall.at[pl.ds(((1 - core) * 4 + z) * 4, 4)]
        arrive(other, wc_recv.at[z])
        weighted_shifts(1 - core, z)
        return z

    @pl.loop(0, 3)
    def _(step):
        z = gather(step)
        q0_ref[...] += jnp.dot(a2_ref[z], t2_ref[...], preferred_element_type=F32)
        q1_ref[...] += jnp.dot(a2_ref[z, :, :256], t2_ref[256:, :], preferred_element_type=F32)

    z = gather(3)
    for part in range(2):
        to_half = ms // 4 if part else 1 - ms // 4
        rows = pl.ds(pl.multiple_of(256 * to_half, 256), 256)
        q0_ref[rows, :] += jnp.dot(a2_ref[z, rows, :], t2_ref[...], preferred_element_type=F32)
        q1_ref[rows, :] += jnp.dot(a2_ref[z, rows, :256], t2_ref[256:, :], preferred_element_type=F32)

        @pl.loop(0, 4)
        def _(r):
            for v in range(6):
                lo, hi = folded(earlier, q0_ref, q1_ref, pl.multiple_of(256 * to_half + 8 * r, 8), 32, v)
                gf[part, r, :, 128 * v : 128 * v + 128] = jnp.concatenate([lo, hi], 0)

        for k in (2, 1, 3, 0):
            to = (ms + k) % 4
            if part and k == 0:
                continue
            slot = to_half * 4 + to
            gmsg[slot] = gf[part, to].astype(BF16)
            sent.append(
                send(gmsg.at[slot], grecv.at[ms], g_send.at[4 * part + k], g_recv.at[ms], sensor_at(slot))
            )

    total = gf[1, ms % 4]
    for k in (1, 3, 2):
        at = (ms // 4) * 4 + (ms + k) % 4
        arrive(grecv.at[at], g_recv.at[at])
        total = total + grecv[at].astype(F32)
    for k in range(4):
        at = (1 - ms // 4) * 4 + (ms + k) % 4
        arrive(grecv.at[at], g_recv.at[at])
        total = total + grecv[at].astype(F32)
    for v in range(6):
        for t in range(2):
            out_ref[8 * v : 8 * v + 8, 128 * t : 128 * t + 128] = total[8 * t : 8 * t + 8, 128 * v : 128 * v + 128]

    for copy in sent:
        copy.wait_send()

    @pl.loop(0, 4)
    def _(b):
        sent_off(ybuf.at[b, 0], c_send.at[b])
        sent_off(wall.at[pl.ds((core * 4 + b) * 4, 4)], wc_send.at[b])
        for dy in range(4):

            @pl.when((b < 3) | (dy > 0))
            def _():
                sent_off(ybuf.at[b, 1, (y + dy) % 4], z_send.at[b, dy])


def shards(histories, kernel, noise_weight):
    V, S = pltpu.VMEM, pltpu.SemaphoreType.DMA
    out = pl.pallas_call(
        body,
        out_shape=jax.ShapeDtypeStruct((48, 256), F32),
        in_specs=[pl.BlockSpec(memory_space=pltpu.HBM)] * 3,
        out_specs=pl.BlockSpec(memory_space=pltpu.VMEM),
        scratch_shapes=[
            V((64, 64, 256), BF16), V((64, 256), F32), V((2, 4608, 128), F32), V((2, 512, 1024), BF16),
            V((1024, 1024), BF16), V((4, 128, 2048), BF16), V((4, 512, 512), BF16), V((2048, 768), BF16),
            V((128, 768), F32), V((128, 768), F32), V((512, 768), BF16), V((512, 768), F32), V((512, 768), F32),
            V((8, 48, 256), BF16), V((4, 2, 4, 8, 384), F32), V((4, 4, 8, 384), F32), V((16, 8, 384), F32),
            V((32, 16, 256), BF16), V((2, 4, 16, 768), F32), V((8, 16, 768), BF16), V((8, 16, 768), BF16),
            S((6,)), S((8,)), S((8,)), S((4,)), S((4,)), S((4, 4)), S((16,)), S((16,)), S((16,)), S((4,)), S((4,)),
            S((8,)), S((8,)),
        ],
        compiler_params=pltpu.CompilerParams(
            collective_id=0, has_side_effects=True, vmem_limit_bytes=60 * 2**20
        ),
        cost_estimate=pl.CostEstimate(flops=4831838208, bytes_accessed=2300000, transcendentals=0),
        name="hessian",
    )(kernel, histories.transpose(1, 0, 2).reshape(48, 256), noise_weight)
    return out.reshape(6, 8, 256).transpose(1, 0, 2)


def solution(mesh):
    in_specs = (P(("param", "sensor"), None, None), P("sensor", "param", None), P("sensor", None))
    out_specs = P(("param", "sensor"), None, None)
    return jax.shard_map(shards, mesh=mesh, in_specs=in_specs, out_specs=out_specs, check_vma=False)
```

time: 50.6 us -> 48.8 us (0.964)
  Pallas kernels: 49 us -> 47.2 us
    pallas_call x1, Pallas kernels: 49 us -> 47.2 us  [shards(): pl.pallas_call(body, out_shape=jax.ShapeDtypeStruct((48, 256), F32), in_s...]
where the time goes in v3:
time: 48.8 us; the launch traced here: 48.7 us
  Pallas kernels  47.2 us (97%)
  local copies, waits for them, and re-layouts  1.42 us (3%)
    pallas_call x1, Pallas kernels, shards(): pl.pallas_call(body, out_shape=jax.ShapeDtypeStruct((48, 256), F32), in_s...  47.2 us
    unnamed x1, local copies, waits for them, and re-layouts  1.42 us

profile of v3, /device:TPU:1, one launch (start us, length us, event | category | flops | bytes accessed | tf_op | source)
XLA Modules:
  0.0 48.7 jit_solution(16864154821858143213)
XLA Ops:
  0.0 47.2 %hessian.1 = f32[48,256]{1,0:T(8,128)} custom-call(bf16[64,64,256]{2,1,0:T(8,128)(2,1)} %k_hbm.1, bf16[48,256]{1,0:T(8,128)(2,1)} %bitcast.7, f32[64,256]{1,0:T(8,128)} %noise_hbm.1), custom_call_target="tpu_custom_call" | custom-call | flops 4831838208 | bytes 2300000 | tf_op jit(solution)/shard_map/hessian/pallas_call | solution.py:340
  47.2 1.4 %copy.5 = f32[8,6,256]{2,0,1:T(8,128)} copy(f32[8,6,256]{2,0,1:T(8,128)} %bitcast.6) | data formatting | bytes 98304

commit v4 on v3

--- a/solution.py
+++ b/solution.py
@@ -116,7 +116,7 @@
     k_hbm, hist_hbm, noise_hbm, out_ref,
     k_ref, noise_ref, wide_ref, x_ref, order_ref, a1_ref, a2_ref, t1_ref, long_ref, short_ref, t2_ref, q0_ref, q1_ref,
     hb, ybuf, yrecv, zrecv, wall, gf, gmsg, grecv,
-    load_sem, h_send, h_recv, c_send, c_recv, z_send, z_recv, w_send, w_recv, wc_send, wc_recv, g_send, g_recv,
+    load_sem, told, h_send, h_recv, c_send, c_recv, z_send, z_recv, w_send, w_recv, wc_send, wc_recv, g_send, g_recv,
 ):
     ms, mp = lax.axis_index("sensor"), lax.axis_index("param")
     zh, y, core = mp // 8, (mp // 2) % 4, mp % 2
@@ -140,13 +140,17 @@
     barrier = pltpu.get_barrier_semaphore()
     peers = [sensor_at((ms + k) % 8) for k in range(1, 8)]
     peers += [partner]
-    peers += [param_at((zh + dz) % 4, (y + dy) % 4, core) for dz in range(4) for dy in range(4) if dz or dy]
+    peers += [param_at(zh, (y + dy) % 4, core) for dy in range(1, 4)]
+    beside = [param_at((zh + dz) % 4, y, core) for dz in (1, 3)]
+    peers += beside
     for peer in peers:
         pl.semaphore_signal(barrier, inc=1, device_id=peer, device_id_type=MESH)
 
     fill_order(order_ref)
     pltpu.make_async_copy(hist_hbm, hb.at[ms], load_sem.at[0]).wait()
     pl.semaphore_wait(barrier, len(peers))
+    for peer in beside:
+        pl.semaphore_signal(told.at[0], inc=1, device_id=peer, device_id_type=MESH)
 
     def send(src, dst, send_sem, recv_sem, peer):
         copy = pltpu.make_async_remote_copy(
@@ -180,6 +184,10 @@
                     wide_ref[h, pl.ds(pl.multiple_of(i * 72, 8), 64), :] = k_ref[i, :, 128 * h : 128 * h + 128].astype(F32)
 
     forward_taps(k_ref, wide_ref, x_ref, order_ref, a1_ref)
+
+    pl.semaphore_wait(told.at[0], 2)
+    for peer in beside:
+        pl.semaphore_signal(told.at[1], inc=1, device_id=peer, device_id_type=MESH)
 
     @pl.loop(0, 8)
     def _(k):
@@ -219,6 +227,10 @@
                 ybuf[b, mine, v // 3, :, col] = lo
                 ybuf[b, mine, 2 + v // 3, :, col] = hi
         send(ybuf.at[b, 0], yrecv.at[b], c_send.at[b], c_recv.at[b], partner)
+
+        @pl.when(b == 1)
+        def _():
+            pl.semaphore_wait(told.at[1], 2)
 
         @pl.when(b > 0)
         def _():
@@ -348,7 +360,7 @@
             V((128, 768), F32), V((128, 768), F32), V((512, 768), BF16), V((512, 768), F32), V((512, 768), F32),
             V((8, 48, 256), BF16), V((4, 2, 4, 8, 384), F32), V((4, 4, 8, 384), F32), V((16, 8, 384), F32),
             V((32, 16, 256), BF16), V((2, 4, 16, 768), F32), V((8, 16, 768), BF16), V((8, 16, 768), BF16),
-            S((6,)), S((8,)), S((8,)), S((4,)), S((4,)), S((4, 4)), S((16,)), S((16,)), S((16,)), S((4,)), S((4,)),
+            S((6,)), pltpu.SemaphoreType.REGULAR((2,)), S((8,)), S((8,)), S((4,)), S((4,)), S((4, 4)), S((16,)), S((16,)), S((16,)), S((4,)), S((4,)),
             S((8,)), S((8,)),
         ],
         compiler_params=pltpu.CompilerParams(

time: 48.8 us -> 45.9 us (0.941)
  Pallas kernels: 47.2 us -> 44.3 us
    pallas_call x1, Pallas kernels: 47.2 us -> 44.3 us  [shards(): pl.pallas_call(body, out_shape=jax.ShapeDtypeStruct((48, 256), F32), in_s...]
where the time goes in v4:
time: 45.9 us; the launch traced here: 45.7 us
  Pallas kernels  44.3 us (97%)
  local copies, waits for them, and re-layouts  1.42 us (3%)
    pallas_call x1, Pallas kernels, shards(): pl.pallas_call(body, out_shape=jax.ShapeDtypeStruct((48, 256), F32), in_s...  44.3 us
    unnamed x1, local copies, waits for them, and re-layouts  1.42 us

profile of v4, /device:TPU:1, one launch (start us, length us, event | category | flops | bytes accessed | tf_op | source)
XLA Modules:
  0.0 45.7 jit_solution(9094413979442139808)
XLA Ops:
  0.0 44.3 %hessian.1 = f32[48,256]{1,0:T(8,128)} custom-call(bf16[64,64,256]{2,1,0:T(8,128)(2,1)} %k_hbm.1, bf16[48,256]{1,0:T(8,128)(2,1)} %bitcast.7, f32[64,256]{1,0:T(8,128)} %noise_hbm.1), custom_call_target="tpu_custom_call" | custom-call | flops 4831838208 | bytes 2300000 | tf_op jit(solution)/shard_map/hessian/pallas_call | solution.py:352
  44.3 1.4 %copy.5 = f32[8,6,256]{2,0,1:T(8,128)} copy(f32[8,6,256]{2,0,1:T(8,128)} %bitcast.6) | data formatting | bytes 98304

commit v5 on v4

--- a/solution.py
+++ b/solution.py
@@ -170,8 +170,9 @@
         ).wait_send()
 
     sent = []
-    for k in (2, 6, 1, 3, 5, 7, 4):
-        sent.append(send(hb.at[ms], hb.at[ms], h_send.at[k], h_recv.at[ms], sensor_at((ms + k) % 8)))
+    for dz, dx in ((1, 2), (1, 1), (1, 3), (0, 2), (1, 0), (0, 1), (0, 3)):
+        peer = sensor_at((ms // 4 + dz) % 2 * 4 + (ms + dx) % 4)
+        sent.append(send(hb.at[ms], hb.at[ms], h_send.at[4 * dz + dx], h_recv.at[ms], peer))
 
     for part in range(4):
         k_loads[part].wait()
@@ -191,7 +192,9 @@
 
     @pl.loop(0, 8)
     def _(k):
-        s = (ms + k) % 8
+        dz = jnp.where(k == 3, 1, k // 5)
+        dx = jnp.where(k == 4, 2, jnp.where(k == 7, 2, jnp.where((k == 1) | (k == 5), 1, jnp.where((k == 2) | (k == 6), 3, 0))))
+        s = (ms // 4 + dz) % 2 * 4 + (ms + dx) % 4
 
         @pl.when(k > 0)
         def _():
@@ -274,8 +277,11 @@
             lo, hi = [pieces[y_][row : row + 8, col : col + 128] for y_ in (v // 3, 2 + v // 3)]
             adjoint_shifts(t2_ref, half, v, lo, hi)
 
-    def gather(step):
-        z = (zh + jnp.where(step == 0, 0, jnp.where(step == 1, 1, jnp.where(step == 2, 3, 2)))) % 4
+    def z_in(step):
+        return (zh + jnp.where(step == 0, 0, jnp.where(step == 1, 1, jnp.where(step == 2, 3, 2)))) % 4
+
+    def fetch(step):
+        z = z_in(step)
         for dy in (1, 3, 2, 0):
             at = (y + dy) % 4
 
@@ -285,21 +291,33 @@
 
         block = wall.at[pl.ds((core * 4 + z) * 4, 4)]
         send(block, block, wc_send.at[z], wc_recv.at[z], partner)
+
+    def other_half(z):
+        arrive(wall.at[pl.ds(((1 - core) * 4 + z) * 4, 4)], wc_recv.at[z])
+        weighted_shifts(1 - core, z)
+
+    fetch(0)
+
+    @pl.loop(0, 4)
+    def _(step):
+        z = z_in(step)
         weighted_shifts(core, z)
-        other = wall.at[pl.ds(((1 - core) * 4 + z) * 4, 4)]
-        arrive(other, wc_recv.at[z])
-        weighted_shifts(1 - core, z)
-        return z
-
-    @pl.loop(0, 3)
-    def _(step):
-        z = gather(step)
-        q0_ref[...] += jnp.dot(a2_ref[z], t2_ref[...], preferred_element_type=F32)
-        q1_ref[...] += jnp.dot(a2_ref[z, :, :256], t2_ref[256:, :], preferred_element_type=F32)
-
-    z = gather(3)
-    for part in range(2):
-        to_half = ms // 4 if part else 1 - ms // 4
+
+        @pl.when(step < 3)
+        def _():
+            fetch(step + 1)
+
+        other_half(z)
+
+        @pl.when(step < 3)
+        def _():
+            q0_ref[...] += jnp.dot(a2_ref[z], t2_ref[...], preferred_element_type=F32)
+            q1_ref[...] += jnp.dot(a2_ref[z, :, :256], t2_ref[256:, :], preferred_element_type=F32)
+
+    @pl.loop(0, 2)
+    def _(part):
+        z = z_in(3)
+        to_half = (ms // 4 + 1 + part) % 2
         rows = pl.ds(pl.multiple_of(256 * to_half, 256), 256)
         q0_ref[rows, :] += jnp.dot(a2_ref[z, rows, :], t2_ref[...], preferred_element_type=F32)
         q1_ref[rows, :] += jnp.dot(a2_ref[z, rows, :256], t2_ref[256:, :], preferred_element_type=F32)
@@ -311,14 +329,12 @@
                 gf[part, r, :, 128 * v : 128 * v + 128] = jnp.concatenate([lo, hi], 0)
 
         for k in (2, 1, 3, 0):
-            to = (ms + k) % 4
-            if part and k == 0:
-                continue
-            slot = to_half * 4 + to
-            gmsg[slot] = gf[part, to].astype(BF16)
-            sent.append(
-                send(gmsg.at[slot], grecv.at[ms], g_send.at[4 * part + k], g_recv.at[ms], sensor_at(slot))
-            )
+            slot = to_half * 4 + (ms + k) % 4
+
+            @pl.when((part == 0) | (k > 0))
+            def _():
+                gmsg[slot] = gf[part, (ms + k) % 4].astype(BF16)
+                send(gmsg.at[slot], grecv.at[ms], g_send.at[slot], g_recv.at[ms], sensor_at(slot))
 
     total = gf[1, ms % 4]
     for k in (1, 3, 2):
@@ -335,6 +351,9 @@
 
     for copy in sent:
         copy.wait_send()
+    for k in range(1, 8):
+        slot = (ms + k) % 8
+        sent_off(gmsg.at[slot], g_send.at[slot])
 
     @pl.loop(0, 4)
     def _(b):

time: 45.9 us -> 44.7 us (0.974)
  Pallas kernels: 44.3 us -> 43.1 us
    pallas_call x1, Pallas kernels: 44.3 us -> 43.1 us  [shards(): pl.pallas_call(body, out_shape=jax.ShapeDtypeStruct((48, 256), F32), in_s...]
where the time goes in v5:
time: 44.7 us; the launch traced here: 44.6 us
  Pallas kernels  43.1 us (96%)
  local copies, waits for them, and re-layouts  1.42 us (3%)
    pallas_call x1, Pallas kernels, shards(): pl.pallas_call(body, out_shape=jax.ShapeDtypeStruct((48, 256), F32), in_s...  43.1 us
    unnamed x1, local copies, waits for them, and re-layouts  1.42 us

profile of v5, /device:TPU:1, one launch (start us, length us, event | category | flops | bytes accessed | tf_op | source)
XLA Modules:
  0.0 44.6 jit_solution(12053085606709869509)
XLA Ops:
  0.0 43.1 %hessian.1 = f32[48,256]{1,0:T(8,128)} custom-call(bf16[64,64,256]{2,1,0:T(8,128)(2,1)} %k_hbm.1, bf16[48,256]{1,0:T(8,128)(2,1)} %bitcast.7, f32[64,256]{1,0:T(8,128)} %noise_hbm.1), custom_call_target="tpu_custom_call" | custom-call | flops 4831838208 | bytes 2300000 | tf_op jit(solution)/shard_map/hessian/pallas_call | solution.py:371
  43.1 1.4 %copy.5 = f32[8,6,256]{2,0,1:T(8,128)} copy(f32[8,6,256]{2,0,1:T(8,128)} %bitcast.6) | data formatting | bytes 98304

commit v6 on v5

--- a/solution.py
+++ b/solution.py
@@ -28,7 +28,7 @@
     return jnp.dot(x, order_ref[:, pl.ds(pl.multiple_of(n * 256, 256), 256)], preferred_element_type=F32)
 
 
-def forward_taps(k_ref, wide_ref, x_ref, order_ref, a_ref):
+def forward_taps(wide_ref, x_ref, order_ref, a_ref, beside, tell):
     for h in range(2):
 
         @pl.loop(0, 8)
@@ -37,8 +37,7 @@
             for j in range(8):
                 x_ref[h, row, 128 * j : 128 * j + 128] = wide_ref[h, pl.ds(8 * g + j, 64, stride=72), :].astype(BF16)
 
-    @pl.loop(0, 8)
-    def _(step):
+    def one(step):
         h, n = step // 4, step % 4
         ys = reordered(x_ref[h], order_ref, n)
         for z in range(4):
@@ -49,6 +48,14 @@
                     row = pl.ds(pl.multiple_of((2 * n + c) * 16, 16), 16)
                     col = pl.ds(pl.multiple_of(h * 1024 + g * 128, 128), 128)
                     a_ref[z, row, col] = jnp.concatenate(part, 0).astype(BF16)
+
+    pl.loop(0, 5)(one)
+    tell()
+
+    @pl.loop(5, 8)
+    def _(step):
+        beside(step)
+        one(step)
 
 
 def adjoint_taps(k_ref, order_ref, a_ref, h):
@@ -174,6 +181,28 @@
         peer = sensor_at((ms // 4 + dz) % 2 * 4 + (ms + dx) % 4)
         sent.append(send(hb.at[ms], hb.at[ms], h_send.at[4 * dz + dx], h_recv.at[ms], peer))
 
+    def sensor_of(k):
+        dz = jnp.where(k == 3, 1, k // 5)
+        dx = jnp.where((k == 4) | (k == 7), 2, jnp.where((k == 1) | (k == 5), 1, jnp.where((k == 2) | (k == 6), 3, 0)))
+        return (ms // 4 + dz) % 2 * 4 + (ms + dx) % 4
+
+    def series_of(s):
+        block = hb[s].astype(F32)
+        for v in range(6):
+            forward_shifts(t1_ref, s, v, block[8 * v : 8 * v + 8, :128], block[8 * v : 8 * v + 8, 128:])
+
+    def series(k):
+        s = sensor_of(k)
+        arrive(hb.at[s], h_recv.at[s])
+        series_of(s)
+
+    series_of(ms)
+
+    def tell():
+        pl.semaphore_wait(told.at[0], 2)
+        for peer in beside:
+            pl.semaphore_signal(told.at[1], inc=1, device_id=peer, device_id_type=MESH)
+
     for part in range(4):
         k_loads[part].wait()
 
@@ -184,25 +213,9 @@
                 for h in range(2):
                     wide_ref[h, pl.ds(pl.multiple_of(i * 72, 8), 64), :] = k_ref[i, :, 128 * h : 128 * h + 128].astype(F32)
 
-    forward_taps(k_ref, wide_ref, x_ref, order_ref, a1_ref)
-
-    pl.semaphore_wait(told.at[0], 2)
-    for peer in beside:
-        pl.semaphore_signal(told.at[1], inc=1, device_id=peer, device_id_type=MESH)
-
-    @pl.loop(0, 8)
-    def _(k):
-        dz = jnp.where(k == 3, 1, k // 5)
-        dx = jnp.where(k == 4, 2, jnp.where(k == 7, 2, jnp.where((k == 1) | (k == 5), 1, jnp.where((k == 2) | (k == 6), 3, 0))))
-        s = (ms // 4 + dz) % 2 * 4 + (ms + dx) % 4
-
-        @pl.when(k > 0)
-        def _():
-            arrive(hb.at[s], h_recv.at[s])
-
-        block = hb[s].astype(F32)
-        for v in range(6):
-            forward_shifts(t1_ref, s, v, block[8 * v : 8 * v + 8, :128], block[8 * v : 8 * v + 8, 128:])
+    forward_taps(wide_ref, x_ref, order_ref, a1_ref, lambda step: series(step - 4), tell)
+
+    pl.loop(4, 8)(series)
 
     def z_of(b):
         return (zh + jnp.where(b == 0, 2, jnp.where(b == 1, 1, jnp.where(b == 2, 3, 0)))) % 4
@@ -323,20 +336,21 @@
         q1_ref[rows, :] += jnp.dot(a2_ref[z, rows, :256], t2_ref[256:, :], preferred_element_type=F32)
 
         @pl.loop(0, 4)
-        def _(r):
+        def _(turn):
+            k = jnp.where(turn == 0, 2, jnp.where(turn == 1, 1, jnp.where(turn == 2, 3, 0)))
+            r = (ms + k) % 4
+            slot = to_half * 4 + r
             for v in range(6):
                 lo, hi = folded(earlier, q0_ref, q1_ref, pl.multiple_of(256 * to_half + 8 * r, 8), 32, v)
-                gf[part, r, :, 128 * v : 128 * v + 128] = jnp.concatenate([lo, hi], 0)
-
-        for k in (2, 1, 3, 0):
-            slot = to_half * 4 + (ms + k) % 4
-
-            @pl.when((part == 0) | (k > 0))
+                both = jnp.concatenate([lo, hi], 0)
+                gf[:, 128 * v : 128 * v + 128] = both
+                gmsg[slot, :, 128 * v : 128 * v + 128] = both.astype(BF16)
+
+            @pl.when((part == 0) | (turn < 3))
             def _():
-                gmsg[slot] = gf[part, (ms + k) % 4].astype(BF16)
                 send(gmsg.at[slot], grecv.at[ms], g_send.at[slot], g_recv.at[ms], sensor_at(slot))
 
-    total = gf[1, ms % 4]
+    total = gf[...]
     for k in (1, 3, 2):
         at = (ms // 4) * 4 + (ms + k) % 4
         arrive(grecv.at[at], g_recv.at[at])
@@ -378,7 +392,7 @@
             V((1024, 1024), BF16), V((4, 128, 2048), BF16), V((4, 512, 512), BF16), V((2048, 768), BF16),
             V((128, 768), F32), V((128, 768), F32), V((512, 768), BF16), V((512, 768), F32), V((512, 768), F32),
             V((8, 48, 256), BF16), V((4, 2, 4, 8, 384), F32), V((4, 4, 8, 384), F32), V((16, 8, 384), F32),
-            V((32, 16, 256), BF16), V((2, 4, 16, 768), F32), V((8, 16, 768), BF16), V((8, 16, 768), BF16),
+            V((32, 16, 256), BF16), V((16, 768), F32), V((8, 16, 768), BF16), V((8, 16, 768), BF16),
             S((6,)), pltpu.SemaphoreType.REGULAR((2,)), S((8,)), S((8,)), S((4,)), S((4,)), S((4, 4)), S((16,)), S((16,)), S((16,)), S((4,)), S((4,)),
             S((8,)), S((8,)),
         ],

time: 44.7 us -> 43.8 us (0.980)
  Pallas kernels: 43.1 us -> 42.2 us
    pallas_call x1, Pallas kernels: 43.1 us -> 42.2 us  [shards(): pl.pallas_call(body, out_shape=jax.ShapeDtypeStruct((48, 256), F32), in_s...]
where the time goes in v6:
time: 43.8 us; the launch traced here: 43.7 us
  Pallas kernels  42.2 us (96%)
  local copies, waits for them, and re-layouts  1.42 us (3%)
    pallas_call x1, Pallas kernels, shards(): pl.pallas_call(body, out_shape=jax.ShapeDtypeStruct((48, 256), F32), in_s...  42.2 us
    unnamed x1, local copies, waits for them, and re-layouts  1.42 us

profile of v6, /device:TPU:1, one launch (start us, length us, event | category | flops | bytes accessed | tf_op | source)
XLA Modules:
  0.0 43.7 jit_solution(8722544552617752808)
XLA Ops:
  0.0 42.2 %hessian.1 = f32[48,256]{1,0:T(8,128)} custom-call(bf16[64,64,256]{2,1,0:T(8,128)(2,1)} %k_hbm.1, bf16[48,256]{1,0:T(8,128)(2,1)} %bitcast.7, f32[64,256]{1,0:T(8,128)} %noise_hbm.1), custom_call_target="tpu_custom_call" | custom-call | flops 4831838208 | bytes 2300000 | tf_op jit(solution)/shard_map/hessian/pallas_call | solution.py:385
  42.3 1.4 %copy.5 = f32[8,6,256]{2,0,1:T(8,128)} copy(f32[8,6,256]{2,0,1:T(8,128)} %bitcast.6) | data formatting | bytes 98304

commit v7 on v6

--- a/solution.py
+++ b/solution.py
@@ -273,7 +273,7 @@
     wall[here] = jnp.concatenate(
         [jnp.concatenate(tiles[:2], 1), jnp.concatenate(tiles[2:], 1)], 0
     ).astype(BF16)
-    for dz in (2, 1, 3, 0):
+    for dz in (0, 2, 1, 3):
         for dy in (2, 1, 3, 0):
             if dz or dy:
                 peer = param_at((zh + dz) % 4, (y + dy) % 4, core)

time: 43.8 us -> 43.9 us (level)
  no operation moved by 1% of the time
where the time goes in v7:
time: 43.9 us; the launch traced here: 43.7 us
  Pallas kernels  42.3 us (96%)
  local copies, waits for them, and re-layouts  1.42 us (3%)
    pallas_call x1, Pallas kernels, shards(): pl.pallas_call(body, out_shape=jax.ShapeDtypeStruct((48, 256), F32), in_s...  42.3 us
    unnamed x1, local copies, waits for them, and re-layouts  1.42 us

profile of v7, /device:TPU:1, one launch (start us, length us, event | category | flops | bytes accessed | tf_op | source)
XLA Modules:
  0.0 43.7 jit_solution(17433229856084684884)
XLA Ops:
  0.0 42.3 %hessian.1 = f32[48,256]{1,0:T(8,128)} custom-call(bf16[64,64,256]{2,1,0:T(8,128)(2,1)} %k_hbm.1, bf16[48,256]{1,0:T(8,128)(2,1)} %bitcast.7, f32[64,256]{1,0:T(8,128)} %noise_hbm.1), custom_call_target="tpu_custom_call" | custom-call | flops 4831838208 | bytes 2300000 | tf_op jit(solution)/shard_map/hessian/pallas_call | solution.py:385
  42.3 1.4 %copy.5 = f32[8,6,256]{2,0,1:T(8,128)} copy(f32[8,6,256]{2,0,1:T(8,128)} %bitcast.6) | data formatting | bytes 98304

commit v8 on v6

--- a/solution.py
+++ b/solution.py
@@ -28,7 +28,7 @@
     return jnp.dot(x, order_ref[:, pl.ds(pl.multiple_of(n * 256, 256), 256)], preferred_element_type=F32)
 
 
-def forward_taps(wide_ref, x_ref, order_ref, a_ref, beside, tell):
+def group_taps(wide_ref, x_ref):
     for h in range(2):
 
         @pl.loop(0, 8)
@@ -37,6 +37,8 @@
             for j in range(8):
                 x_ref[h, row, 128 * j : 128 * j + 128] = wide_ref[h, pl.ds(8 * g + j, 64, stride=72), :].astype(BF16)
 
+
+def forward_taps(wide_ref, x_ref, order_ref, a_ref, beside, tell):
     def one(step):
         h, n = step // 4, step % 4
         ys = reordered(x_ref[h], order_ref, n)
@@ -154,6 +156,17 @@
         pl.semaphore_signal(barrier, inc=1, device_id=peer, device_id_type=MESH)
 
     fill_order(order_ref)
+    for part in range(4):
+        k_loads[part].wait()
+
+        @pl.loop(8 * part, 8 * part + 8)
+        def _(step):
+            for u in range(2):
+                i = 2 * step + u
+                for h in range(2):
+                    wide_ref[h, pl.ds(pl.multiple_of(i * 72, 8), 64), :] = k_ref[i, :, 128 * h : 128 * h + 128].astype(F32)
+
+    group_taps(wide_ref, x_ref)
     pltpu.make_async_copy(hist_hbm, hb.at[ms], load_sem.at[0]).wait()
     pl.semaphore_wait(barrier, len(peers))
     for peer in beside:
@@ -202,16 +215,6 @@
         pl.semaphore_wait(told.at[0], 2)
         for peer in beside:
             pl.semaphore_signal(told.at[1], inc=1, device_id=peer, device_id_type=MESH)
-
-    for part in range(4):
-        k_loads[part].wait()
-
-        @pl.loop(8 * part, 8 * part + 8)
-        def _(step):
-            for u in range(2):
-                i = 2 * step + u
-                for h in range(2):
-                    wide_ref[h, pl.ds(pl.multiple_of(i * 72, 8), 64), :] = k_ref[i, :, 128 * h : 128 * h + 128].astype(F32)
 
     forward_taps(wide_ref, x_ref, order_ref, a1_ref, lambda step: series(step - 4), tell)
 

time: 43.8 us -> 44.4 us (1.014)
  Pallas kernels: 42.2 us -> 42.8 us
    pallas_call x1, Pallas kernels: 42.2 us -> 42.8 us  [shards(): pl.pallas_call(body, out_shape=jax.ShapeDtypeStruct((48, 256), F32), in_s...]
where the time goes in v8:
time: 44.4 us; the launch traced here: 44.3 us
  Pallas kernels  42.8 us (96%)
  local copies, waits for them, and re-layouts  1.42 us (3%)
    pallas_call x1, Pallas kernels, shards(): pl.pallas_call(body, out_shape=jax.ShapeDtypeStruct((48, 256), F32), in_s...  42.8 us
    unnamed x1, local copies, waits for them, and re-layouts  1.42 us

profile of v8, /device:TPU:1, one launch (start us, length us, event | category | flops | bytes accessed | tf_op | source)
XLA Modules:
  0.0 44.3 jit_solution(16804919727713732997)
XLA Ops:
  0.0 42.8 %hessian.1 = f32[48,256]{1,0:T(8,128)} custom-call(bf16[64,64,256]{2,1,0:T(8,128)(2,1)} %k_hbm.1, bf16[48,256]{1,0:T(8,128)(2,1)} %bitcast.7, f32[64,256]{1,0:T(8,128)} %noise_hbm.1), custom_call_target="tpu_custom_call" | custom-call | flops 4831838208 | bytes 2300000 | tf_op jit(solution)/shard_map/hessian/pallas_call | solution.py:388
  42.8 1.4 %copy.5 = f32[8,6,256]{2,0,1:T(8,128)} copy(f32[8,6,256]{2,0,1:T(8,128)} %bitcast.6) | data formatting | bytes 98304
